TPU v7x, 32 devices: a whole 2x2x4 slice. The times are simulated.
32 devices in a mesh: dp: 16 (over z, y, core), book: 2 (over x).
Axes of the slice: x: 2, y: 2, z: 4, core: 2. Of those that a mesh axis runs over, the one named last changes fastest.
Arguments:
- corpus_rows: bfloat16 [12288, 1024], P('dp'), may hold values from -6 to 6
- code_ids: int32 [12288, 8], P('dp', 'book'), may hold values from 0 to 2047
- master: float32 [8, 2048, 1024], P('book', 'dp'), may hold values from -5 to 5
- first_moment: float32 [8, 2048, 1024], P('book', 'dp'), may hold values from -6 to 6
- second_moment: float32 [8, 2048, 1024], P('book', 'dp'), may hold values from 1 to 30
Outputs:
- new_master: float32 [8, 2048, 1024], P('book', 'dp')
- new_first: float32 [8, 2048, 1024], P('book', 'dp')
- new_second: float32 [8, 2048, 1024], P('book', 'dp')
All inputs are finite; a program needn't handle non-finite values.
Results may differ from a plain program's by a relative error of at most 0.002.
Values may be sent and summed in bfloat16 or wider, within the bound.
A program may use at most 192 MiB of HBM per device.

v0:
```python
import jax
import jax.numpy as jnp
from jax import lax
from jax.sharding import PartitionSpec as P

STEPS = 2


def make_pull(corpus_rows, recon):
    values = corpus_rows.astype(jnp.float32)
    resid = values - recon
    unit = values * lax.rsqrt(jnp.sum(values * values, axis=-1, keepdims=True) + 1e-06)
    along = jnp.sum(resid * unit, axis=-1, keepdims=True)
    return (resid + 3.0 * along * unit).astype(jnp.bfloat16)


def per_device(corpus_rows, code_ids, master, first_moment, second_moment):
    book_count = master.shape[0]
    shard_rows = master.shape[1]
    width = master.shape[2]
    local_rows = corpus_rows.shape[0]
    for turn_index in range(STEPS):
        books = master.astype(jnp.bfloat16)
        empty = jnp.zeros((local_rows, width), jnp.float32)
        full_books = lax.all_gather(books, "dp", axis=1, tiled=True)
        partial_value = empty
        for book_slot in range(book_count):
            partial_value = partial_value + jnp.take(
                full_books[book_slot], code_ids[:, book_slot], axis=0
            ).astype(jnp.float32)
        recon = lax.psum(partial_value, "book")
        pull = make_pull(corpus_rows, recon)
        columns = lax.broadcasted_iota(jnp.int32, (1, lax.axis_size("dp") * shard_rows), 1)
        blocks = []
        for grad_book_slot in range(book_count):
            one_hot = (code_ids[:, grad_book_slot][:, None] == columns).astype(jnp.bfloat16)
            summed = lax.dot_general(
                one_hot, pull, (((0,), (0,)), ((), ())), preferred_element_type=jnp.float32
            )
            blocks.append(-2.0 * summed)
        grad_flat = lax.psum_scatter(
            jnp.concatenate(blocks, axis=1), "dp", scatter_dimension=0, tiled=True
        )
        grad = jnp.transpose(grad_flat.reshape(shard_rows, book_count, width), (1, 0, 2))
        first_moment = 0.9 * first_moment + 0.1 * grad
        second_moment = 0.99 * second_moment + 0.01 * grad * grad
        master = master - 0.05 * first_moment / (jnp.sqrt(second_moment) + 1e-08)
    return (master, first_moment, second_moment)


def solution(mesh):
    in_specs = (
        P("dp", None),
        P("dp", "book"),
        P("book", "dp", None),
        P("book", "dp", None),
        P("book", "dp", None),
    )
    out_specs = (P("book", "dp", None), P("book", "dp", None), P("book", "dp", None))
    return jax.shard_map(
        per_device, mesh=mesh, in_specs=in_specs, out_specs=out_specs, check_vma=False
    )
```

profile of v0, /device:TPU:0, one launch (start us, length us, event | category | flops | bytes accessed | tf_op | source)
XLA Modules:
  0.0 1295.0 jit_solution(10355159778973246720)
XLA Ops:
  7.2 0.0 all-gather.3.cloned.1.call-start
  7.2 2.7 convert_element_type.49
  10.0 0.0 all-reduce.3.cloned.1.call-start
  10.2 130.2 %all-gather.3.cloned.1.call-done = bf16[4,2048,1024]{2,1,0:T(8,128)(2,1)} async-done(((bf16[4,128,1024]{2,1,0:T(8,128)(2,1)}), bf16[4,2048,1024]{2,1,0:T(8,128)(2,1)}) %all-gather.3.cloned.1.call-update) | async-done | bytes 16777232 | tf_op jit(solution)/shard_map/all_gather | solution.py:25
  140.4 12.2 slice_bitcast_fusion.7
  152.6 6.5 gather_fusion
  159.2 6.5 gather_fusion.3
  165.7 7.3 gather_fusion.2
  173.0 7.3 gather_fusion.1
  180.3 4.0 convert_add_fusion.1
  184.3 0.0 all-reduce.3.cloned.1.call-update
  184.3 0.2 reduce-scatter.3.cloned.1.call-start
  184.6 1.2 copy-done
  185.7 0.4 fusion.26
  186.1 82.3 %all-reduce.3.cloned.1.call-done = f32[768,1024]{1,0:T(8,128)} async-done(((f32[768,1024]{1,0:T(8,128)}), f32[768,1024]{1,0:T(8,128)}) %all-reduce.3.cloned.1.call-update) | async-done | bytes 3145744 | tf_op jit(solution)/shard_map/psum | solution.py:31
  268.4 2.8 fusion.20
  271.2 0.0 copy-done.2
  271.2 0.7 fusion.22
  271.9 3.8 fusion.18
  275.7 3.8 fusion.16
  279.5 6.2 fusion.14
  285.7 6.0 fusion.12
  291.7 18.8 %pad_maximum_fusion = f32[2048,4096]{0,1:T(8,128)} fusion(f32[2048,1024]{0,1:T(8,128)S(1)} %fusion.18, f32[2048,1024]{0,1:T(8,128)S(1)} %fusion.16, f32[2048,1024]{0,1:T(8,128)} %fusion.14, f32[2048,1024]{0,1:T(8,128)} %fusion.12), kind=kLoop, calls=%fused_computation.8 | loop fusion | flops 25165824 | bytes 67108864 | tf_op jit(solution)/shard_map/concatenate | solution.py:42
  310.6 0.0 all-gather.5.cloned.1.call-start
  310.6 332.9 %reduce-scatter.3.cloned.1.call-done = f32[128,4096]{0,1:T(8,128)} async-done(((f32[2048,4096]{0,1:T(8,128)}), f32[128,4096]{0,1:T(8,128)}) %reduce-scatter.3.cloned.1.call-update) | async-done | bytes 2097168 | tf_op jit(solution)/shard_map/reduce_scatter | solution.py:41
  643.5 2.9 copy.8
  646.4 6.5 fusion.41
  652.9 0.0 all-reduce.5.cloned.1.call-start
  652.9 126.0 %all-gather.5.cloned.1.call-done = bf16[4,2048,1024]{2,1,0:T(8,128)(2,1)} async-done(((bf16[4,128,1024]{2,1,0:T(8,128)(2,1)}), bf16[4,2048,1024]{2,1,0:T(8,128)(2,1)}) %all-gather.5.cloned.1.call-update) | async-done | bytes 16777232 | tf_op jit(solution)/shard_map/all_gather | solution.py:25
  778.9 12.6 slice_bitcast_fusion.3
  791.5 6.5 gather_fusion.4
  798.0 7.3 gather_fusion.7
  805.3 7.3 gather_fusion.6
  812.6 7.3 gather_fusion.5
  819.9 4.3 convert_add_fusion
  824.2 0.2 reduce-scatter.5.cloned.1.call-start
  824.5 83.9 %all-reduce.5.cloned.1.call-done = f32[768,1024]{1,0:T(8,128)} async-done(((f32[768,1024]{1,0:T(8,128)}), f32[768,1024]{1,0:T(8,128)}) %all-reduce.5.cloned.1.call-update) | async-done | bytes 3145744 | tf_op jit(solution)/shard_map/psum | solution.py:31
  908.3 2.8 fusion.23
  911.1 0.0 copy-done.3
  911.2 0.7 fusion.25
  911.9 3.8 fusion.19
  915.6 3.8 fusion.17
  919.4 4.0 fusion.15
  923.4 6.0 fusion.13
  929.4 14.9 %pad_maximum_fusion.1 = f32[2048,4096]{0,1:T(8,128)} fusion(f32[2048,1024]{0,1:T(8,128)S(1)} %fusion.19, f32[2048,1024]{0,1:T(8,128)S(1)} %fusion.17, f32[2048,1024]{0,1:T(8,128)S(1)} %fusion.15, f32[2048,1024]{0,1:T(8,128)} %fusion.13), kind=kLoop, calls=%fused_computation.9 | loop fusion | flops 25165824 | bytes 67108864 | tf_op jit(solution)/shard_map/concatenate | solution.py:42
  944.3 332.9 %reduce-scatter.5.cloned.1.call-done = f32[128,4096]{0,1:T(8,128)} async-done(((f32[2048,4096]{0,1:T(8,128)}), f32[128,4096]{0,1:T(8,128)}) %reduce-scatter.5.cloned.1.call-update) | async-done | bytes 2097168 | tf_op jit(solution)/shard_map/reduce_scatter | solution.py:41
  1277.2 3.0 copy.9
  1280.3 7.6 divide_subtract_fusion
  (24 shorter events, 0.2 us)
Async XLA Ops:
  7.2 2.9 copy-start.4
  7.2 133.3 %all-gather.3.cloned.1.call-start = ((), (), s32[]{:S(2)}) async-start(), calls=%async_computation.2 | async-start | bytes 17825792 | tf_op jit(solution)/shard_map/all_gather | solution.py:25
  10.0 258.4 %all-reduce.3.cloned.1.call-start = ((), (), s32[]{:S(2)}) async-start(), calls=%async_computation.3 | async-start | bytes 6291456 | tf_op jit(solution)/shard_map/psum | solution.py:31
  184.3 1.4 copy-start
  184.3 459.1 %reduce-scatter.3.cloned.1.call-start = ((), (), s32[]{:S(2)}) async-start(), calls=%async_computation.4 | async-start | bytes 35651584 | tf_op jit(solution)/shard_map/reduce_scatter | solution.py:41
  268.4 2.8 copy-start.2
  310.6 468.4 %all-gather.5.cloned.1.call-start = ((), (), s32[]{:S(2)}) async-start(), calls=%async_computation.5 | async-start | bytes 17825792 | tf_op jit(solution)/shard_map/all_gather | solution.py:25
  652.9 255.5 %all-reduce.5.cloned.1.call-start = ((), (), s32[]{:S(2)}) async-start(), calls=%async_computation.6 | async-start | bytes 6291456 | tf_op jit(solution)/shard_map/psum | solution.py:31
  824.2 453.0 %reduce-scatter.5.cloned.1.call-start = ((), (), s32[]{:S(2)}) async-start(), calls=%async_computation.7 | async-start | bytes 35651584 | tf_op jit(solution)/shard_map/reduce_scatter | solution.py:41
  908.3 2.8 copy-start.3
  1277.2 3.0 copy-start.1
Sparse Core Ops, SparseCore 0:
  10.8 129.6 all-gather.2
  184.5 83.9 all-reduce.2
  310.7 332.7 reduce-scatter.2
  653.0 125.9 all-gather.4
  824.4 83.9 all-reduce.4
  944.5 332.7 reduce-scatter.4
where the time goes:
time: 1300 us; the launch traced here: 1290 us
  waiting for transfers between devices  1090 us (84%)
  local copies, waits for them, and re-layouts  88 us (7%)
  other arithmetic  66.3 us (5%)
  matrix products  37.3 us (3%)
  between operations  14.5 us (1%)
    reduce_scatter x2, waiting for transfers between devices, per_device(): lax.psum_scatter(jnp.concatenate(blocks, axis=1), 'dp', scatter_dimension...  666 us
    all_gather x2, waiting for transfers between devices, per_device(): full_books = lax.all_gather(books, 'dp', axis=1, tiled=True)  256 us
    psum x2, waiting for transfers between devices, per_device(): recon = lax.psum(partial_value, 'book')  166 us
    gather x8, local copies, waits for them, and re-layouts, per_device(): jnp.take(full_books[book_slot], code_ids[:, book_slot], axis=0)  56 us
    dot_general x8, matrix products, per_device(): lax.dot_general(one_hot, pull, (((0,), (0,)), ((), ())), preferred_elemen...  37.3 us
    concatenate x2, other arithmetic, per_device(): jnp.concatenate(blocks, axis=1)  33.7 us
  transfers between devices with their start and end apart: 6, of which 6 were waited for; matrix products, arithmetic and copies ran while one was open for 0% of the time, Pallas kernels for 0%

commit v1 on v0

--- a/solution.py
+++ b/solution.py
@@ -28,7 +28,7 @@
             partial_value = partial_value + jnp.take(
                 full_books[book_slot], code_ids[:, book_slot], axis=0
             ).astype(jnp.float32)
-        recon = lax.psum(partial_value, "book")
+        recon = jnp.sum(lax.all_gather(partial_value, "book"), axis=0)
         pull = make_pull(corpus_rows, recon)
         columns = lax.broadcasted_iota(jnp.int32, (1, lax.axis_size("dp") * shard_rows), 1)
         blocks = []

time: 1300 us -> 1300 us (level)
    psum x2 -> x0, waiting for transfers between devices: 166 us -> none  [per_device(): recon = lax.psum(partial_value, 'book')]
    all_gather x0 -> x2, waiting for transfers between devices: none -> 155 us  [per_device(): recon = jnp.sum(lax.all_gather(partial_value, 'book'), axis=0)]
where the time goes in v1:
time: 1300 us
  waiting for transfers between devices  1080 us (83%)
  local copies, waits for them, and re-layouts  88 us (7%)
  other arithmetic  77.3 us (6%)
  matrix products  37.3 us (3%)
  between operations  14.5 us (1%)
    reduce_scatter x2, waiting for transfers between devices, per_device(): lax.psum_scatter(jnp.concatenate(blocks, axis=1), 'dp', scatter_dimension...  666 us
    all_gather x2, waiting for transfers between devices, per_device(): full_books = lax.all_gather(books, 'dp', axis=1, tiled=True)  256 us
    all_gather x2, waiting for transfers between devices, per_device(): recon = jnp.sum(lax.all_gather(partial_value, 'book'), axis=0)  155 us
    gather x8, local copies, waits for them, and re-layouts, per_device(): jnp.take(full_books[book_slot], code_ids[:, book_slot], axis=0)  56 us
    dot_general x8, matrix products, per_device(): lax.dot_general(one_hot, pull, (((0,), (0,)), ((), ())), preferred_elemen...  37.3 us
    concatenate x2, other arithmetic, per_device(): jnp.concatenate(blocks, axis=1)  33.7 us
  transfers between devices with their start and end apart: 6, of which 6 were waited for; matrix products, arithmetic and copies ran while one was open for 0% of the time, Pallas kernels for 0%

profile of v1, /device:TPU:0, one launch (start us, length us, event | category | flops | bytes accessed | tf_op | source)
XLA Modules:
  0.0 1295.3 jit_solution(6842992515241666089)
XLA Ops:
  7.2 0.0 all-gather.7.cloned.1.call-start
  7.2 2.7 convert_element_type.49
  10.0 0.0 all-gather.11.cloned.1.call-start
  10.2 130.2 %all-gather.7.cloned.1.call-done = bf16[4,2048,1024]{2,1,0:T(8,128)(2,1)} async-done(((bf16[4,128,1024]{2,1,0:T(8,128)(2,1)}), bf16[4,2048,1024]{2,1,0:T(8,128)(2,1)}) %all-gather.7.cloned.1.call-update) | async-done | bytes 16777232 | tf_op jit(solution)/shard_map/all_gather | solution.py:25
  140.4 12.2 slice_bitcast_fusion.7
  152.6 6.5 gather_fusion
  159.2 6.5 gather_fusion.3
  165.7 7.3 gather_fusion.2
  173.0 7.3 gather_fusion.1
  180.3 4.1 convert_add_fusion.1
  184.4 0.2 reduce-scatter.3.cloned.1.call-start
  184.6 1.2 copy-done
  185.8 0.4 fusion.26
  186.2 76.9 %all-gather.11.cloned.1.call-done = f32[1536,1024]{1,0:T(8,128)} async-done(((f32[768,1024]{1,0:T(8,128)}), f32[1536,1024]{1,0:T(8,128)}) %all-gather.11.cloned.1.call-update) | async-done | bytes 6291472 | tf_op jit(solution)/shard_map/all_gather | solution.py:31
  263.1 5.4 reduce_sum.49
  268.5 2.8 fusion.20
  271.4 0.7 fusion.22
  272.1 3.8 fusion.18
  275.8 3.8 fusion.16
  279.6 6.2 fusion.14
  285.9 6.0 fusion.12
  291.8 18.8 %pad_maximum_fusion = f32[2048,4096]{0,1:T(8,128)} fusion(f32[2048,1024]{0,1:T(8,128)S(1)} %fusion.18, f32[2048,1024]{0,1:T(8,128)S(1)} %fusion.16, f32[2048,1024]{0,1:T(8,128)} %fusion.14, f32[2048,1024]{0,1:T(8,128)} %fusion.12), kind=kLoop, calls=%fused_computation.8 | loop fusion | flops 25165824 | bytes 67108864 | tf_op jit(solution)/shard_map/concatenate | solution.py:42
  310.7 0.0 all-gather.9.cloned.1.call-start
  310.7 332.8 %reduce-scatter.3.cloned.1.call-done = f32[128,4096]{0,1:T(8,128)} async-done(((f32[2048,4096]{0,1:T(8,128)}), f32[128,4096]{0,1:T(8,128)}) %reduce-scatter.3.cloned.1.call-update) | async-done | bytes 2097168 | tf_op jit(solution)/shard_map/reduce_scatter | solution.py:41
  643.6 2.9 copy.8
  646.4 6.5 fusion.41
  653.0 0.0 all-gather.13.cloned.1.call-start
  653.0 126.1 %all-gather.9.cloned.1.call-done = bf16[4,2048,1024]{2,1,0:T(8,128)(2,1)} async-done(((bf16[4,128,1024]{2,1,0:T(8,128)(2,1)}), bf16[4,2048,1024]{2,1,0:T(8,128)(2,1)}) %all-gather.9.cloned.1.call-update) | async-done | bytes 16777232 | tf_op jit(solution)/shard_map/all_gather | solution.py:25
  779.1 12.6 slice_bitcast_fusion.3
  791.7 6.5 gather_fusion.4
  798.2 7.3 gather_fusion.7
  805.5 7.3 gather_fusion.6
  812.8 7.3 gather_fusion.5
  820.1 4.4 convert_add_fusion
  824.5 0.2 reduce-scatter.5.cloned.1.call-start
  824.7 78.5 %all-gather.13.cloned.1.call-done = f32[1536,1024]{1,0:T(8,128)} async-done(((f32[768,1024]{1,0:T(8,128)}), f32[1536,1024]{1,0:T(8,128)}) %all-gather.13.cloned.1.call-update) | async-done | bytes 6291472 | tf_op jit(solution)/shard_map/all_gather | solution.py:31
  903.2 5.4 reduce_sum.52
  908.6 2.8 fusion.23
  911.4 0.0 copy-done.1
  911.5 0.7 fusion.25
  912.2 3.8 fusion.19
  915.9 3.8 fusion.17
  919.7 4.0 fusion.15
  923.7 6.0 fusion.13
  929.7 14.9 %pad_maximum_fusion.1 = f32[2048,4096]{0,1:T(8,128)} fusion(f32[2048,1024]{0,1:T(8,128)S(1)} %fusion.19, f32[2048,1024]{0,1:T(8,128)S(1)} %fusion.17, f32[2048,1024]{0,1:T(8,128)S(1)} %fusion.15, f32[2048,1024]{0,1:T(8,128)} %fusion.13), kind=kLoop, calls=%fused_computation.9 | loop fusion | flops 25165824 | bytes 67108864 | tf_op jit(solution)/shard_map/concatenate | solution.py:42
  944.7 332.9 %reduce-scatter.5.cloned.1.call-done = f32[128,4096]{0,1:T(8,128)} async-done(((f32[2048,4096]{0,1:T(8,128)}), f32[128,4096]{0,1:T(8,128)}) %reduce-scatter.5.cloned.1.call-update) | async-done | bytes 2097168 | tf_op jit(solution)/shard_map/reduce_scatter | solution.py:41
  1277.6 3.0 copy.9
  1280.6 7.6 divide_subtract_fusion
  (26 shorter events, 0.2 us)
Async XLA Ops:
  7.2 2.9 copy-start.4
  7.2 133.3 %all-gather.7.cloned.1.call-start = ((), (), s32[]{:S(2)}) async-start(), calls=%async_computation.2 | async-start | bytes 17825792 | tf_op jit(solution)/shard_map/all_gather | solution.py:25
  10.0 253.1 %all-gather.11.cloned.1.call-start = ((), (), s32[]{:S(2)}) async-start(), calls=%async_computation.6 | async-start | bytes 9437184 | tf_op jit(solution)/shard_map/all_gather | solution.py:31
  184.4 1.4 copy-start
  184.4 459.2 %reduce-scatter.3.cloned.1.call-start = ((), (), s32[]{:S(2)}) async-start(), calls=%async_computation.3 | async-start | bytes 35651584 | tf_op jit(solution)/shard_map/reduce_scatter | solution.py:41
  268.5 2.8 copy-start.2
  310.7 468.4 %all-gather.9.cloned.1.call-start = ((), (), s32[]{:S(2)}) async-start(), calls=%async_computation.4 | async-start | bytes 17825792 | tf_op jit(solution)/shard_map/all_gather | solution.py:25
  653.0 250.2 %all-gather.13.cloned.1.call-start = ((), (), s32[]{:S(2)}) async-start(), calls=%async_computation.7 | async-start | bytes 9437184 | tf_op jit(solution)/shard_map/all_gather | solution.py:31
  824.5 453.1 %reduce-scatter.5.cloned.1.call-start = ((), (), s32[]{:S(2)}) async-start(), calls=%async_computation.5 | async-start | bytes 35651584 | tf_op jit(solution)/shard_map/reduce_scatter | solution.py:41
  908.6 2.8 copy-start.1
  1277.6 3.0 copy-start.3
Sparse Core Ops, SparseCore 0:
  10.8 129.6 all-gather.6
  184.5 78.5 all-gather.10
  310.8 332.7 reduce-scatter.2
  653.1 125.9 all-gather.8
  824.6 78.5 all-gather.12
  944.8 332.7 reduce-scatter.4
